TPU v7x, 512 devices: a whole 4x8x8 slice. The times are simulated.
512 devices in a mesh: traj: 32 (over x, y), cand: 16 (over z, core).
Axes of the slice: x: 4, y: 8, z: 8, core: 2. Of those that a mesh axis runs over, the one named last changes fastest.
Arguments:
- state: float32 [4096, 256], P('traj'), may hold values from -6 to 6
- target: float32 [4096, 256], P('traj'), may hold values from -6 to 6
- coeffs: bfloat16 [33280, 256], P('cand'), may hold values from -6 to 6
- pairs: int32 [2, 33280], P(None, 'cand'), may hold values from 0 to 256, as said below
- mask: int32 [33280, 256], P('cand'), may hold values 0 or 1
Outputs:
- slope: float32 [4096, 256], P('traj')
- new_coeffs: bfloat16 [33280, 256], P('cand')
Inputs may be any that keep to these rules, and one draw needn't show every extreme that they name: Each column holds a pair pairs[0, c] <= pairs[1, c]; index 256 stands for the constant 1; no pair repeats before every pair has appeared.
All inputs are finite; a program needn't handle non-finite values. No bound on the sum of `mask` on one device may be relied on, other than what follows from the above.
Results may differ from a plain program's by a relative error of at most 0.014.
Values may be sent and summed in bfloat16 or wider, within the bound.
No kernel may reach another device: no remote copies, remote signals or barrier semaphores. Data moves between devices by JAX's collectives and lax.ppermute only.
A program may use at most 64 MiB of HBM per device.

v0:
```python
import math
import jax
import jax.numpy as jnp
from jax import lax
from jax.sharding import PartitionSpec as P

CANDS = 33280
step_dt = 0.25


def body(state, target, coeffs, pairs, mask):
    rows, modes_count = state.shape
    left = pairs[0]
    right = pairs[1]
    scale = 1.0 / math.sqrt(CANDS)
    segments = rows * lax.axis_size("traj")
    modes = jnp.arange(modes_count, dtype=jnp.int32)
    jac_left = (left[:, None] == modes[None, :]).astype(jnp.bfloat16)
    jac_right = (right[:, None] == modes[None, :]).astype(jnp.bfloat16)
    ones_col = jnp.ones((rows, 1), jnp.float32)

    def factors(y):
        z = jnp.concatenate([y, ones_col], 1)
        return (jnp.take(z, left, axis=1), jnp.take(z, right, axis=1))

    def library(y):
        left_vals, right_vals = factors(y)
        return (left_vals * right_vals).astype(jnp.bfloat16)

    def derive(theta):
        partial_rate = jnp.dot(theta, coeffs, preferred_element_type=jnp.float32) * scale
        return lax.psum(partial_rate, "cand")

    def pullback(cot, y):
        hidden = (
            lax.dot_general(
                cot.astype(jnp.bfloat16),
                coeffs,
                (((1,), (1,)), ((), ())),
                preferred_element_type=jnp.float32,
            )
            * scale
        )
        left_vals, right_vals = factors(y)
        upper = (hidden * right_vals).astype(jnp.bfloat16)
        lower = (hidden * left_vals).astype(jnp.bfloat16)
        partial_cot = jnp.dot(upper, jac_left, preferred_element_type=jnp.float32)
        partial_cot = partial_cot + jnp.dot(lower, jac_right, preferred_element_type=jnp.float32)
        return lax.psum(partial_cot, "cand")

    y_two = None
    th1 = library(state)
    k1 = derive(th1)
    y_two = state + 0.5 * step_dt * k1
    th2 = library(y_two)
    k2 = derive(th2)
    y_three = state + 0.5 * step_dt * k2
    th3 = library(y_three)
    k3 = derive(th3)
    y_four = state + step_dt * k3
    th4 = library(y_four)
    k4 = derive(th4)
    slope = (k1 + 2.0 * k2 + 2.0 * k3 + k4) / 6.0
    cot = (state + step_dt * slope - target) / segments
    g4 = step_dt / 6.0 * cot
    c4 = pullback(g4, y_four)
    g3 = step_dt / 3.0 * cot + step_dt * c4
    c3 = pullback(g3, y_three)
    g2 = step_dt / 3.0 * cot + 0.5 * step_dt * c3
    c2 = pullback(g2, y_two)
    g1 = step_dt / 6.0 * cot + 0.5 * step_dt * c2

    def outer(theta, grad_cot):
        return lax.dot_general(
            theta,
            grad_cot.astype(jnp.bfloat16),
            (((0,), (0,)), ((), ())),
            preferred_element_type=jnp.float32,
        )

    grad = (outer(th1, g1) + outer(th2, g2) + outer(th3, g3) + outer(th4, g4)) * scale
    rate = 0.5 * math.sqrt(segments * CANDS) / step_dt
    total = lax.psum(grad, "traj")
    fresh = (mask.astype(jnp.float32) * (coeffs.astype(jnp.float32) - rate * total)).astype(
        jnp.bfloat16
    )
    return (slope, fresh)


def solution(mesh):
    placed = (P("traj", None), P("traj", None), P("cand", None), P(None, "cand"), P("cand", None))
    return jax.shard_map(
        body,
        mesh=mesh,
        in_specs=placed,
        out_specs=(P("traj", None), P("cand", None)),
        check_vma=False,
    )
```

profile of v0, /device:TPU:16, one launch (start us, length us, event | category | flops | bytes accessed | tf_op | source)
XLA Modules:
  0.0 1064.3 jit_solution(13873290852304407379)
XLA Ops:
  9.1 3.9 gather_fusion.1
  13.1 5.1 gather_fusion
  18.2 3.0 fusion.19
  21.2 1.0 convolution_multiply_fusion.6
  22.2 118.2 %all-reduce.13.cloned.1.call-done = f32[128,256]{1,0:T(8,128)} async-done(((f32[128,256]{1,0:T(8,128)}), f32[128,256]{1,0:T(8,128)}) %all-reduce.13.cloned.1.call-update) | async-done | bytes 131088 | tf_op jit(solution)/shard_map/psum | solution.py:32
  141.5 3.9 gather_fusion.3
  145.4 3.9 gather_fusion.2
  149.4 1.4 fusion.16
  151.6 1.0 convolution_multiply_fusion.5
  152.7 113.5 %all-reduce.15.cloned.1.call-done = f32[128,256]{1,0:T(8,128)} async-done(((f32[128,256]{1,0:T(8,128)}), f32[128,256]{1,0:T(8,128)}) %all-reduce.15.cloned.1.call-update) | async-done | bytes 131088 | tf_op jit(solution)/shard_map/psum | solution.py:32
  268.8 5.1 gather_fusion.5
  273.9 5.0 gather_fusion.4
  278.9 3.1 fusion.13
  282.8 1.0 convolution_multiply_fusion.4
  283.9 113.5 %all-reduce.17.cloned.1.call-done = f32[128,256]{1,0:T(8,128)} async-done(((f32[128,256]{1,0:T(8,128)}), f32[128,256]{1,0:T(8,128)}) %all-reduce.17.cloned.1.call-update) | async-done | bytes 131088 | tf_op jit(solution)/shard_map/psum | solution.py:32
  400.0 5.1 gather_fusion.7
  405.1 5.0 gather_fusion.6
  410.1 3.1 fusion.10
  414.0 1.0 convolution_multiply_fusion.3
  415.1 113.5 %all-reduce.19.cloned.1.call-done = f32[128,256]{1,0:T(8,128)} async-done(((f32[128,256]{1,0:T(8,128)}), f32[128,256]{1,0:T(8,128)}) %all-reduce.19.cloned.1.call-update) | async-done | bytes 131088 | tf_op jit(solution)/shard_map/psum | solution.py:32
  528.6 1.9 add_subtract_fusion
  532.9 1.7 fusion.7
  534.7 113.5 %all-reduce.21.cloned.1.call-done = f32[128,256]{1,0:T(8,128)} async-done(((f32[128,256]{1,0:T(8,128)}), f32[128,256]{1,0:T(8,128)}) %all-reduce.21.cloned.1.call-update) | async-done | bytes 131088 | tf_op jit(solution)/shard_map/psum | solution.py:49
  651.6 1.7 fusion.8
  653.5 113.3 %all-reduce.23.cloned.1.call-done = f32[128,256]{1,0:T(8,128)} async-done(((f32[128,256]{1,0:T(8,128)}), f32[128,256]{1,0:T(8,128)}) %all-reduce.23.cloned.1.call-update) | async-done | bytes 131088 | tf_op jit(solution)/shard_map/psum | solution.py:49
  769.2 1.7 fusion.9
  771.0 113.5 %all-reduce.25.cloned.1.call-done = f32[128,256]{1,0:T(8,128)} async-done(((f32[128,256]{1,0:T(8,128)}), f32[128,256]{1,0:T(8,128)}) %all-reduce.25.cloned.1.call-update) | async-done | bytes 131088 | tf_op jit(solution)/shard_map/psum | solution.py:49
  884.5 1.3 fusion.44
  885.8 1.5 convolution_add_fusion.2
  888.4 1.8 fusion
  890.9 163.6 %all-reduce.27.cloned.1.call-done = f32[2080,256]{1,0:T(8,128)} async-done(((f32[2080,256]{1,0:T(8,128)}), f32[2080,256]{1,0:T(8,128)}) %all-reduce.27.cloned.1.call-update) | async-done | bytes 2129936 | tf_op jit(solution)/shard_map/psum | solution.py:83
  1054.5 3.0 multiply_convert_fusion
  (72 shorter events, 21.0 us)
Async XLA Ops:
  7.2 133.3 %all-reduce.13.cloned.1.call-start = ((), (), s32[]{:S(2)}) async-start(), calls=%async_computation | async-start | bytes 262144 | tf_op jit(solution)/shard_map/psum | solution.py:32
  18.1 3.0 copy-start
  21.1 120.2 %copy-start.10 = (bf16[128,2080]{0,1:T(8,128)(2,1)}, bf16[128,2080]{0,1:T(8,128)(2,1)S(1)}, u32[]{:S(2)}) copy-start(bf16[128,2080]{0,1:T(8,128)(2,1)S(1)} %fusion.19) | copy-start | bytes 1597444
  21.1 119.3 %copy-start.12 = (f32[128,256]{1,0:T(8,128)S(1)}, f32[128,256]{1,0:T(8,128)}, u32[]{:S(2)}) copy-start(f32[128,256]{1,0:T(8,128)} %param.7) | copy-start | bytes 393220
  22.2 244.0 %all-reduce.15.cloned.1.call-start = ((), (), s32[]{:S(2)}) async-start(), calls=%async_computation.1 | async-start | bytes 262144 | tf_op jit(solution)/shard_map/psum | solution.py:32
  150.8 0.8 copy-start.5
  152.6 244.8 %all-reduce.17.cloned.1.call-start = ((), (), s32[]{:S(2)}) async-start(), calls=%async_computation.2 | async-start | bytes 262144 | tf_op jit(solution)/shard_map/psum | solution.py:32
  282.0 0.8 copy-start.6
  283.8 244.8 %all-reduce.19.cloned.1.call-start = ((), (), s32[]{:S(2)}) async-start(), calls=%async_computation.3 | async-start | bytes 262144 | tf_op jit(solution)/shard_map/psum | solution.py:32
  413.2 0.8 copy-start.8
  415.0 233.2 %all-reduce.21.cloned.1.call-start = ((), (), s32[]{:S(2)}) async-start(), calls=%async_computation.4 | async-start | bytes 262144 | tf_op jit(solution)/shard_map/psum | solution.py:49
  530.5 1.2 copy-start.4
  531.7 1.2 copy-start.3
  534.6 232.2 %all-reduce.23.cloned.1.call-start = ((), (), s32[]{:S(2)}) async-start(), calls=%async_computation.5 | async-start | bytes 262144 | tf_op jit(solution)/shard_map/psum | solution.py:49
  649.1 1.2 copy-start.2
  650.4 1.2 copy-start.1
  653.3 231.2 %all-reduce.25.cloned.1.call-start = ((), (), s32[]{:S(2)}) async-start(), calls=%async_computation.6 | async-start | bytes 262144 | tf_op jit(solution)/shard_map/psum | solution.py:49
  769.2 115.3 %copy-start.11 = (bf16[128,2080]{0,1:T(8,128)(2,1)S(1)}, bf16[128,2080]{0,1:T(8,128)(2,1)}, u32[]{:S(2)}) copy-start(bf16[128,2080]{0,1:T(8,128)(2,1)} %copy-done.10) | copy-start | bytes 1597444
  770.9 283.5 %all-reduce.27.cloned.1.call-start = ((), (), s32[]{:S(2)}) async-start(), calls=%async_computation.7 | async-start | bytes 4259840 | tf_op jit(solution)/shard_map/psum | solution.py:83
  885.8 1.5 copy-start.7
  887.4 1.0 copy-start.9
  888.4 1.8 copy-start.14
  890.2 164.3 %copy-start.13 = (s32[2080,256]{1,0:T(8,128)S(1)}, s32[2080,256]{1,0:T(8,128)}, u32[]{:S(2)}) copy-start(s32[2080,256]{1,0:T(8,128)} %param.11) | copy-start | bytes 6389764
Sparse Core Ops, SparseCore 0:
  22.3 118.0 all-reduce.12
  152.7 113.4 all-reduce.14
  284.0 113.4 all-reduce.16
  415.2 113.4 all-reduce.18
  534.8 113.4 all-reduce.20
  653.4 113.4 all-reduce.22
  771.0 113.3 all-reduce.24
  890.3 164.0 all-reduce.26
where the time goes:
time: 1060 us
  waiting for transfers between devices  963 us (91%)
  local copies, waits for them, and re-layouts  47.4 us (4%)
  other arithmetic  20.6 us (2%)
  matrix products  18.4 us (2%)
  between operations  14.5 us (1%)
    psum x4, waiting for transfers between devices, derive(): return lax.psum(partial_rate, 'cand')  459 us
    psum x3, waiting for transfers between devices, pullback(): return lax.psum(partial_cot, 'cand')  340 us
    psum x1, waiting for transfers between devices, body(): total = lax.psum(grad, 'traj')  164 us
    gather x8, local copies, waits for them, and re-layouts, factors(): return (jnp.take(z, left, axis=1), jnp.take(z, right, axis=1))  37.1 us
  transfers between devices with their start and end apart: 8, of which 8 were waited for; matrix products, arithmetic and copies ran while one was open for 0% of the time, Pallas kernels for 0%

commit v1 on v0

--- a/solution.py
+++ b/solution.py
@@ -80,7 +80,9 @@
 
     grad = (outer(th1, g1) + outer(th2, g2) + outer(th3, g3) + outer(th4, g4)) * scale
     rate = 0.5 * math.sqrt(segments * CANDS) / step_dt
-    total = lax.psum(grad, "traj")
+    total = grad
+    for hop in (1, 2, 4, 8, 16):
+        total = total + lax.ppermute(total, "traj", [(dev, dev ^ hop) for dev in range(32)])
     fresh = (mask.astype(jnp.float32) * (coeffs.astype(jnp.float32) - rate * total)).astype(
         jnp.bfloat16
     )

time: 1060 us -> 1240 us (1.17)
  the two profiles are of different devices: /device:TPU:16 before, /device:TPU:26 now
where the time goes in v1:
time: 1240 us
  waiting for transfers between devices  1130 us (91%)
  local copies, waits for them, and re-layouts  48 us (4%)
  other arithmetic  20.4 us (2%)
  starting transfers between devices  16.5 us (1%)
  matrix products  16 us (1%)
  between operations  14.5 us (1%)
    psum x4, waiting for transfers between devices, derive(): return lax.psum(partial_rate, 'cand')  459 us
    psum x3, waiting for transfers between devices, pullback(): return lax.psum(partial_cot, 'cand')  340 us
    ppermute x5, waiting for transfers between devices, body(): lax.ppermute(total, 'traj', [(dev, dev ^ hop) for dev in range(32)])  329 us
    gather x8, local copies, waits for them, and re-layouts, factors(): return (jnp.take(z, left, axis=1), jnp.take(z, right, axis=1))  37 us
  transfers between devices with their start and end apart: 12, of which 12 were waited for; matrix products, arithmetic and copies ran while one was open for 0% of the time, Pallas kernels for 0%

profile of v1, /device:TPU:26, one launch (start us, length us, event | category | flops | bytes accessed | tf_op | source)
XLA Modules:
  0.0 1243.2 jit_solution(16439905081397876517)
XLA Ops:
  9.1 3.9 gather_fusion.1
  13.1 5.1 gather_fusion
  18.2 3.0 fusion.19
  22.2 118.1 %all-reduce.12.cloned.1.call-done = f32[128,256]{1,0:T(8,128)} async-done(((f32[128,256]{1,0:T(8,128)}), f32[128,256]{1,0:T(8,128)}) %all-reduce.12.cloned.1.call-update) | async-done | bytes 131088 | tf_op jit(solution)/shard_map/psum | solution.py:32
  141.4 3.9 gather_fusion.3
  145.3 3.9 gather_fusion.2
  152.5 113.5 %all-reduce.14.cloned.1.call-done = f32[128,256]{1,0:T(8,128)} async-done(((f32[128,256]{1,0:T(8,128)}), f32[128,256]{1,0:T(8,128)}) %all-reduce.14.cloned.1.call-update) | async-done | bytes 131088 | tf_op jit(solution)/shard_map/psum | solution.py:32
  268.7 5.1 gather_fusion.5
  273.7 5.0 gather_fusion.4
  278.8 3.1 fusion.13
  283.8 113.5 %all-reduce.16.cloned.1.call-done = f32[128,256]{1,0:T(8,128)} async-done(((f32[128,256]{1,0:T(8,128)}), f32[128,256]{1,0:T(8,128)}) %all-reduce.16.cloned.1.call-update) | async-done | bytes 131088 | tf_op jit(solution)/shard_map/psum | solution.py:32
  399.9 5.0 gather_fusion.7
  404.9 5.0 gather_fusion.6
  409.9 3.1 fusion.10
  414.9 113.5 %all-reduce.18.cloned.1.call-done = f32[128,256]{1,0:T(8,128)} async-done(((f32[128,256]{1,0:T(8,128)}), f32[128,256]{1,0:T(8,128)}) %all-reduce.18.cloned.1.call-update) | async-done | bytes 131088 | tf_op jit(solution)/shard_map/psum | solution.py:32
  528.5 1.9 add_subtract_fusion
  532.8 1.6 fusion.7
  534.5 113.5 %all-reduce.20.cloned.1.call-done = f32[128,256]{1,0:T(8,128)} async-done(((f32[128,256]{1,0:T(8,128)}), f32[128,256]{1,0:T(8,128)}) %all-reduce.20.cloned.1.call-update) | async-done | bytes 131088 | tf_op jit(solution)/shard_map/psum | solution.py:49
  651.4 1.7 fusion.8
  653.3 113.4 %all-reduce.22.cloned.1.call-done = f32[128,256]{1,0:T(8,128)} async-done(((f32[128,256]{1,0:T(8,128)}), f32[128,256]{1,0:T(8,128)}) %all-reduce.22.cloned.1.call-update) | async-done | bytes 131088 | tf_op jit(solution)/shard_map/psum | solution.py:49
  769.1 1.7 fusion.9
  770.7 113.6 %all-reduce.24.cloned.1.call-done = f32[128,256]{1,0:T(8,128)} async-done(((f32[128,256]{1,0:T(8,128)}), f32[128,256]{1,0:T(8,128)}) %all-reduce.24.cloned.1.call-update) | async-done | bytes 131088 | tf_op jit(solution)/shard_map/psum | solution.py:49
  888.2 2.4 collective-permute-start
  890.7 47.6 %collective-permute-done = f32[2080,256]{1,0:T(8,128)S(1)} collective-permute-done((f32[2080,256]{1,0:T(8,128)S(1)}, f32[2080,256]{1,0:T(8,128)S(1)}, u32[]{:S(2)}, u32[]{:S(2)}) %collective-permute-start) | collective-permute-done | bytes 2129952 | tf_op jit(solution)/shard_map/ppermute | solution.py:85
  938.6 2.4 collective-permute-start.1
  941.0 93.3 %collective-permute-done.1 = f32[2080,256]{1,0:T(8,128)S(1)} collective-permute-done((f32[2080,256]{1,0:T(8,128)S(1)}, f32[2080,256]{1,0:T(8,128)S(1)}, u32[]{:S(2)}, u32[]{:S(2)}) %collective-permute-start.1) | collective-permute-done | bytes 2129952 | tf_op jit(solution)/shard_map/ppermute | solution.py:85
  1034.6 4.7 collective-permute-start.2
  1039.3 93.8 %collective-permute-done.2 = f32[2080,256]{1,0:T(8,128)S(1)} collective-permute-done((f32[2080,256]{1,0:T(8,128)S(1)}, f32[2080,256]{1,0:T(8,128)S(1)}, u32[]{:S(2)}, u32[]{:S(2)}) %collective-permute-start.2) | collective-permute-done | bytes 2129952 | tf_op jit(solution)/shard_map/ppermute | solution.py:85
  1133.4 2.6 collective-permute-start.3
  1136.0 47.7 %collective-permute-done.3 = f32[2080,256]{1,0:T(8,128)S(1)} collective-permute-done((f32[2080,256]{1,0:T(8,128)S(1)}, f32[2080,256]{1,0:T(8,128)S(1)}, u32[]{:S(2)}, u32[]{:S(2)}) %collective-permute-start.3) | collective-permute-done | bytes 2129952 | tf_op jit(solution)/shard_map/ppermute | solution.py:85
  1183.9 3.9 collective-permute-start.4
  1188.5 46.2 %collective-permute-done.4 = f32[2080,256]{1,0:T(8,128)S(1)} collective-permute-done((f32[2080,256]{1,0:T(8,128)S(1)}, f32[2080,256]{1,0:T(8,128)S(1)}, u32[]{:S(2)}, u32[]{:S(2)}) %collective-permute-start.4) | collective-permute-done | bytes 2129952 | tf_op jit(solution)/shard_map/ppermute | solution.py:85
  (85 shorter events, 32.0 us)
Async XLA Ops:
  7.2 133.1 %all-reduce.12.cloned.1.call-start = ((), (), s32[]{:S(2)}) async-start(), calls=%async_computation | async-start | bytes 262144 | tf_op jit(solution)/shard_map/psum | solution.py:32
  18.1 3.0 copy-start
  21.1 120.1 %copy-start.11 = (bf16[128,2080]{0,1:T(8,128)(2,1)}, bf16[128,2080]{0,1:T(8,128)(2,1)S(1)}, u32[]{:S(2)}) copy-start(bf16[128,2080]{0,1:T(8,128)(2,1)S(1)} %fusion.19) | copy-start | bytes 1597444
  21.1 119.2 %copy-start.13 = (f32[128,256]{1,0:T(8,128)S(1)}, f32[128,256]{1,0:T(8,128)}, u32[]{:S(2)}) copy-start(f32[128,256]{1,0:T(8,128)} %param.7) | copy-start | bytes 393220
  22.2 243.9 %all-reduce.14.cloned.1.call-start = ((), (), s32[]{:S(2)}) async-start(), calls=%async_computation.1 | async-start | bytes 262144 | tf_op jit(solution)/shard_map/psum | solution.py:32
  150.7 0.8 copy-start.5
  152.5 244.8 %all-reduce.16.cloned.1.call-start = ((), (), s32[]{:S(2)}) async-start(), calls=%async_computation.2 | async-start | bytes 262144 | tf_op jit(solution)/shard_map/psum | solution.py:32
  281.8 0.8 copy-start.7
  283.7 244.8 %all-reduce.18.cloned.1.call-start = ((), (), s32[]{:S(2)}) async-start(), calls=%async_computation.3 | async-start | bytes 262144 | tf_op jit(solution)/shard_map/psum | solution.py:32
  413.0 0.8 copy-start.9
  414.9 233.1 %all-reduce.20.cloned.1.call-start = ((), (), s32[]{:S(2)}) async-start(), calls=%async_computation.4 | async-start | bytes 262144 | tf_op jit(solution)/shard_map/psum | solution.py:49
  530.3 1.2 copy-start.4
  531.6 1.2 copy-start.3
  534.5 232.2 %all-reduce.22.cloned.1.call-start = ((), (), s32[]{:S(2)}) async-start(), calls=%async_computation.5 | async-start | bytes 262144 | tf_op jit(solution)/shard_map/psum | solution.py:49
  649.0 1.2 copy-start.2
  650.2 1.2 copy-start.1
  653.1 231.2 %all-reduce.24.cloned.1.call-start = ((), (), s32[]{:S(2)}) async-start(), calls=%async_computation.6 | async-start | bytes 262144 | tf_op jit(solution)/shard_map/psum | solution.py:49
  769.0 115.3 %copy-start.12 = (bf16[128,2080]{0,1:T(8,128)(2,1)S(1)}, bf16[128,2080]{0,1:T(8,128)(2,1)}, u32[]{:S(2)}) copy-start(bf16[128,2080]{0,1:T(8,128)(2,1)} %copy-done.11) | copy-start | bytes 1597444
  884.3 1.4 copy-start.6
  885.7 1.0 copy-start.8
  886.8 1.0 copy-start.10
  888.2 50.1 %collective-permute-start = (f32[2080,256]{1,0:T(8,128)S(1)}, f32[2080,256]{1,0:T(8,128)S(1)}, u32[]{:S(2)}, u32[]{:S(2)}) collective-permute-start(f32[2080,256]{1,0:T(8,128)S(1)} %fusion), channel_id=1, source_target_pairs={{0,16},{16,0},{32,48},{48,32},{64,80},{80,64},{96,112},{112,96},{1... | collective-permute-start | bytes 6389768 | tf_op jit(solution)/shard_map/ppermute | solution.py:85
  938.6 95.8 %collective-permute-start.1 = (f32[2080,256]{1,0:T(8,128)S(1)}, f32[2080,256]{1,0:T(8,128)S(1)}, u32[]{:S(2)}, u32[]{:S(2)}) collective-permute-start(f32[2080,256]{1,0:T(8,128)S(1)} %add.107), channel_id=1, source_target_pairs={{0,32},{16,48},{32,0},{48,16},{64,96},{80,112},{96,64},{112,80},{1... | collective-permute-start | bytes 6389768 | tf_op jit(solution)/shard_map/ppermute | solution.py:85
  1034.6 98.5 %collective-permute-start.2 = (f32[2080,256]{1,0:T(8,128)S(1)}, f32[2080,256]{1,0:T(8,128)S(1)}, u32[]{:S(2)}, u32[]{:S(2)}) collective-permute-start(f32[2080,256]{1,0:T(8,128)S(1)} %add.108), channel_id=1, source_target_pairs={{0,64},{16,80},{32,96},{48,112},{64,0},{80,16},{96,32},{112,48},{1... | collective-permute-start | bytes 6389768 | tf_op jit(solution)/shard_map/ppermute | solution.py:85
  1133.4 54.5 %copy-start.15 = (f32[128,256]{1,0:T(8,128)S(1)}, f32[128,256]{1,0:T(8,128)}, u32[]{:S(2)}) copy-start(f32[128,256]{1,0:T(8,128)} %get-tuple-element.6) | copy-start | bytes 393220
  1133.4 50.2 %collective-permute-start.3 = (f32[2080,256]{1,0:T(8,128)S(1)}, f32[2080,256]{1,0:T(8,128)S(1)}, u32[]{:S(2)}, u32[]{:S(2)}) collective-permute-start(f32[2080,256]{1,0:T(8,128)S(1)} %add.109), channel_id=1, source_target_pairs={{0,128},{16,144},{32,160},{48,176},{64,192},{80,208},{96,224},{112... | collective-permute-start | bytes 6389768 | tf_op jit(solution)/shard_map/ppermute | solution.py:85
  1183.6 51.2 %copy-start.14 = (s32[2080,256]{1,0:T(8,128)S(1)}, s32[2080,256]{1,0:T(8,128)}, u32[]{:S(2)}) copy-start(s32[2080,256]{1,0:T(8,128)} %param.11) | copy-start | bytes 6389764
  1183.9 50.9 %collective-permute-start.4 = (f32[2080,256]{1,0:T(8,128)S(1)}, f32[2080,256]{1,0:T(8,128)S(1)}, u32[]{:S(2)}, u32[]{:S(2)}) collective-permute-start(f32[2080,256]{1,0:T(8,128)S(1)} %add.110), channel_id=1, source_target_pairs={{0,256},{16,272},{32,288},{48,304},{64,320},{80,336},{96,352},{112... | collective-permute-start | bytes 6389768 | tf_op jit(solution)/shard_map/ppermute | solution.py:85
Sparse Core Ops, SparseCore 0:
  22.3 117.9 all-reduce.11
  152.6 113.4 all-reduce.13
  283.8 113.4 all-reduce.15
  415.0 113.4 all-reduce.17
  534.6 113.4 all-reduce.19
  653.2 113.4 all-reduce.21
  770.9 113.4 all-reduce.23
